TPU v7x, 128 devices: a whole 4x4x4 slice. The times are simulated.
128 devices in a mesh: row: 16 (over z_hi, x, core), tm: 8 (over z_lo, y).
Axes of the slice: x: 4, y: 4, z: 4 (z_hi: 2, z_lo: 2; z = z_hi * 2 + z_lo), core: 2. Of those that a mesh axis runs over, the one named last changes fastest.
Arguments:
- snapshots: bfloat16 [8192, 163840], P('tm', 'row'), may hold values from -9 to 9
Outputs:
- lag_gram: float32 [8192, 1123], P(('tm', 'row'))
All inputs are finite; a program needn't handle non-finite values.
Results may differ from a plain program's by a relative error of at most 0.0003.
Values may be sent and summed in bfloat16 or wider, within the bound.
A program may use at most 128 MiB of HBM per device.

v0:
```python
import jax
import jax.numpy as jnp
from jax import lax
from jax.sharding import PartitionSpec as P

LAG = 100


def from_behind(block, axis, distance):
    devices = range(lax.axis_size(axis))
    route = [(i - distance, i) for i in devices if i - distance in devices]
    return lax.ppermute(block, axis, route)


def lagged(left, right):
    return jnp.dot(left, right.T, preferred_element_type=jnp.float32)


def on_device(snapshots):
    leading = snapshots[: LAG - 1]
    strip = from_behind(leading, "tm", -1)
    groups = lax.axis_size("row")
    total_rows = snapshots.shape[1] * groups
    owned_rows = snapshots.shape[0] // groups
    extended = jnp.concatenate([snapshots, strip], axis=0)
    summed = lax.psum(lagged(snapshots, extended), "row")
    start = lax.axis_index("row") * owned_rows
    mine = lax.dynamic_slice_in_dim(summed, start, owned_rows, 0)
    return mine * (1.0 / total_rows)


def solution(mesh):
    in_specs = (P("tm", "row"),)
    out_specs = P(("tm", "row"), None)
    return jax.shard_map(
        on_device, mesh=mesh, in_specs=in_specs, out_specs=out_specs, check_vma=False
    )
```

profile of v0, /device:TPU:1, one launch (start us, length us, event | category | flops | bytes accessed | tf_op | source)
XLA Modules:
  0.0 257.0 jit_solution(14801453401291692068)
XLA Ops:
  6.5 0.0 all-reduce.2.cloned.1.call-start
  6.5 1.7 slice.3
  8.3 1.3 collective-permute-start
  9.6 48.4 %collective-permute-done = bf16[99,10240]{1,0:T(8,128)(2,1)S(1)} collective-permute-done((bf16[99,10240]{1,0:T(8,128)(2,1)S(1)}, bf16[99,10240]{1,0:T(8,128)(2,1)S(1)}, u32[]{:S(2)}, u32[]{:S(2)}) %collective-permute-start) | collective-permute-done | bytes 2027552 | tf_op jit(solution)/shard_map/ppermute | solution.py:12
  58.0 33.6 %fusion.4 = f32[1024,1123]{1,0:T(8,128)} fusion(bf16[1024,10240]{1,0:T(8,128)(2,1)} %param.1, bf16[99,10240]{1,0:T(8,128)(2,1)S(1)} %collective-permute-done), kind=kOutput, calls=%fused_computation.4 | convolution fusion | flops 23597015040 | bytes 27598848 | tf_op jit(solution)/shard_map/dot_general | solution.py:16
  91.5 0.0 all-reduce.2.cloned.1.call-update
  91.6 156.9 %all-reduce.2.cloned.1.call-done = f32[1024,1123]{1,0:T(8,128)} async-done(((f32[1024,1123]{1,0:T(8,128)}), f32[1024,1123]{1,0:T(8,128)}) %all-reduce.2.cloned.1.call-update) | async-done | bytes 4599824 | tf_op jit(solution)/shard_map/psum | solution.py:26
  248.5 1.7 dynamic-slice_multiply_fusion
Async XLA Ops:
  6.5 242.0 %all-reduce.2.cloned.1.call-start = ((), (), s32[]{:S(2)}) async-start(), calls=%async_computation | async-start | bytes 9437184 | tf_op jit(solution)/shard_map/psum | solution.py:26
  8.3 49.7 %collective-permute-start = (bf16[99,10240]{1,0:T(8,128)(2,1)S(1)}, bf16[99,10240]{1,0:T(8,128)(2,1)S(1)}, u32[]{:S(2)}, u32[]{:S(2)}) collective-permute-start(bf16[99,10240]{1,0:T(8,128)(2,1)S(1)} %slice.3), channel_id=1, source_target_pairs={{1,0},{2,1},{3,2},{4,3},{5,4},{6,5},{7,6},{9,8},{10,9},{11,10},{12... | collective-permute-start | bytes 6082568 | tf_op jit(solution)/shard_map/ppermute | solution.py:12
Sparse Core Ops, SparseCore 0:
  91.7 156.7 all-reduce.1
where the time goes:
time: 257 us
  waiting for transfers between devices  205 us (80%)
  matrix products  33.6 us (13%)
  between operations  13.4 us (5%)
    psum x1, waiting for transfers between devices, on_device(): summed = lax.psum(lagged(snapshots, extended), 'row')  157 us
    ppermute x1, waiting for transfers between devices, from_behind(): return lax.ppermute(block, axis, route)  48.4 us
    dot_general x1, matrix products, lagged(): return jnp.dot(left, right.T, preferred_element_type=jnp.float32)  33.6 us
  transfers between devices with their start and end apart: 2, of which 2 were waited for; matrix products, arithmetic and copies ran while one was open for 0% of the time, Pallas kernels for 0%

commit v1 on v0

v1 whole, which is shorter than its diff:
```python
import functools

import jax
import jax.numpy as jnp
from jax import lax
from jax.experimental import pallas as pl
from jax.experimental.pallas import tpu as pltpu
from jax.sharding import PartitionSpec as P

MESH = pl.DeviceIdType.MESH
LAG = 100
CHIPS = 8
TM = 8
TILE = 256
BULK = 96
REST = LAG - 1 - BULK
PIECES = 5
SLOT = 128
CHUNKS = 20
NT = (((1,), (1,)), ((), ()))


def outer(left, right):
    return lax.dot_general(left, right, NT, preferred_element_type=jnp.float32)


def kernel(
    a_ref,
    out_ref,
    a_v,
    tail_v,
    packed_src,
    packed_dst,
    strip,
    acc,
    acc_s,
    pair,
    pair_s,
    part,
    part_s,
    got,
    got_s,
    load_sem,
    tail_sem,
    strip_send,
    strip_recv,
    packed_sem,
    pair_send,
    pair_recv,
    got_send,
    got_recv,
):
    depth = a_v.shape[1]
    groups = acc.shape[0]
    row, tm = lax.axis_index("row"), lax.axis_index("tm")
    chip, core = row // 2, row % 2
    partner = (chip * 2 + 1 - core, tm)
    before = (row, (tm + TM - 1) % TM)
    after = (row, (tm + 1) % TM)

    def peer(other):
        return (other * 2 + core, tm)

    tail = pltpu.make_async_copy(a_ref.at[pl.ds(BULK, 16)], tail_v, tail_sem)
    tail.start()

    def load(block):
        rows = pl.ds(block * TILE, TILE)
        return pltpu.make_async_copy(a_ref.at[rows], a_v.at[rows], load_sem.at[block])

    for block in range(groups):
        load(block).start()

    barrier = pltpu.get_barrier_semaphore()
    pl.semaphore_signal(barrier, inc=1, device_id=partner, device_id_type=MESH)
    for d in range(1, CHIPS):
        pl.semaphore_signal(
            barrier, inc=1, device_id=peer((chip + d) % CHIPS), device_id_type=MESH
        )

    @pl.when(tm > 0)
    def _():
        pl.semaphore_signal(barrier, inc=1, device_id=before, device_id_type=MESH)

    @pl.when(tm < TM - 1)
    def _():
        pl.semaphore_signal(barrier, inc=1, device_id=after, device_id_type=MESH)

    tail.wait()
    piece = depth // PIECES
    rows16 = lax.broadcasted_iota(jnp.int32, (16, piece), 0)
    packed = jnp.zeros((16, piece), jnp.float32)
    for p in range(PIECES):
        x = tail_v[:, p * piece : (p + 1) * piece].astype(jnp.float32)
        x = jnp.where(rows16 < REST, x, 0.0)
        packed += x if p == 0 else pltpu.roll(x, REST * p, 0)
    packed_src[...] = packed.astype(jnp.bfloat16)

    inner = (tm > 0).astype(jnp.int32) + (tm < TM - 1).astype(jnp.int32)
    pl.semaphore_wait(barrier, CHIPS + inner)

    width = depth // CHUNKS

    def send_strip(i):
        cols = pl.ds(pl.multiple_of(i * width, width), width)
        return pltpu.make_async_remote_copy(
            src_ref=a_ref.at[pl.ds(0, BULK), cols],
            dst_ref=strip.at[pl.ds(0, BULK), cols],
            send_sem=strip_send.at[i],
            recv_sem=strip_recv.at[i],
            device_id=before,
            device_id_type=MESH,
        )

    send_packed = pltpu.make_async_remote_copy(
        src_ref=packed_src,
        dst_ref=packed_dst,
        send_sem=packed_sem.at[0],
        recv_sem=packed_sem.at[1],
        device_id=before,
        device_id_type=MESH,
    )

    @pl.when(tm > 0)
    def _():
        send_packed.start()

        def go(i, _):
            send_strip(i).start()
            return 0

        lax.fori_loop(0, CHUNKS, go, 0)

    acc_s[...] = jnp.zeros_like(acc_s)
    strip[pl.ds(112, 16), :] = jnp.zeros((16, depth), jnp.bfloat16)

    def to_pair(g, src, dst):
        return pltpu.make_async_remote_copy(
            src_ref=src.at[:, 1 - core],
            dst_ref=dst,
            send_sem=pair_send.at[g],
            recv_sem=pair_recv.at[g],
            device_id=partner,
            device_id_type=MESH,
        )

    def pair_of(g):
        return to_pair(g, acc.at[g], pair.at[g])

    def to_chip(g, src, dst, d):
        other = (chip + d) % CHIPS
        return pltpu.make_async_remote_copy(
            src_ref=src.at[other],
            dst_ref=dst.at[chip],
            send_sem=got_send.at[g, d],
            recv_sem=got_recv.at[g, d],
            device_id=peer(other),
            device_id_type=MESH,
        )

    def exchange(g, total, from_pair, src, dst, copy):
        copy.wait_recv()
        for q in range(CHIPS):
            src[q] = total[q, core] + from_pair[q]
        for d in range(1, CHIPS):
            to_chip(g, src, dst, d).start()

    def collect(g, src, dst, cols):
        total = src[chip]
        for d in range(1, CHIPS):
            to_chip(g, src, dst, d).wait_recv()
            total += dst[(chip + CHIPS - d) % CHIPS]
        out_ref[:, cols] = total

    def exchange_group(g):
        exchange(g, acc.at[g], pair.at[g], part.at[g], got.at[g], pair_of(g))

    def collect_group(g):
        collect(g, part.at[g], got.at[g], pl.ds(g * TILE, TILE))

    own = TILE // 128
    for block in range(groups):
        load(block).wait()
        rows = pl.ds(block * TILE, TILE)
        tile = outer(a_v[rows, :], a_v[pl.ds(0, TILE), :])
        acc[0, pl.ds(block * own, own)] = tile.reshape(own, 2, 64, TILE)
    pair_of(0).start()
    for g in range(1, groups):
        tile = outer(a_v[...], a_v[pl.ds(g * TILE, TILE), :])
        acc[g] = tile.reshape(CHIPS, 2, 64, TILE)
        pair_of(g).start()
        exchange_group(g - 1)

    def strip_chunk(i):
        cols = pl.ds(pl.multiple_of(i * width, width), width)
        send_strip(i).wait_recv()
        tile = outer(a_v[:, cols], strip[:, cols])
        acc_s[...] += tile.reshape(CHIPS, 2, 64, SLOT)

    @pl.when(tm < TM - 1)
    def _():
        send_packed.wait_recv()
        packed = packed_dst[...].astype(jnp.float32)
        for p in range(PIECES):
            x = packed if p == 0 else pltpu.roll(packed, 16 - REST * p, 0)
            x = jnp.where(rows16 < REST, x, 0.0)
            strip[pl.ds(BULK, 16), pl.ds(p * piece, piece)] = x.astype(jnp.bfloat16)

        strip_chunk(0)

    exchange_group(groups - 1)

    @pl.when(tm < TM - 1)
    def _():
        def early(i, _):
            strip_chunk(i)
            return 0

        lax.fori_loop(1, CHUNKS // 2, early, 0)

    for g in range(groups - 1):
        collect_group(g)

    @pl.when(tm < TM - 1)
    def _():
        def late(i, _):
            strip_chunk(i)
            return 0

        lax.fori_loop(CHUNKS // 2, CHUNKS, late, 0)

    pair_s_copy = to_pair(groups, acc_s, pair_s)
    pair_s_copy.start()
    collect_group(groups - 1)
    exchange(groups, acc_s, pair_s, part_s, got_s, pair_s_copy)
    collect(groups, part_s, got_s, pl.ds(groups * TILE, SLOT))

    @pl.when(tm > 0)
    def _():
        send_packed.wait_send()

        def done(i, _):
            send_strip(i).wait_send()
            return 0

        lax.fori_loop(0, CHUNKS, done, 0)

    for g in range(groups):
        pair_of(g).wait_send()
    pair_s_copy.wait_send()
    for d in range(1, CHIPS):
        for g in range(groups):
            to_chip(g, part.at[g], got.at[g], d).wait_send()
        to_chip(groups, part_s, got_s, d).wait_send()


def on_device(snapshots):
    snap, depth = snapshots.shape
    groups = snap // TILE
    mine = snap // lax.axis_size("row")
    total_rows = depth * lax.axis_size("row")
    columns = snap + LAG - 1
    f32, bf16 = jnp.float32, jnp.bfloat16
    dma = pltpu.SemaphoreType.DMA
    summed = pl.pallas_call(
        kernel,
        out_shape=jax.ShapeDtypeStruct((mine, snap + SLOT), f32),
        in_specs=[pl.BlockSpec(memory_space=pl.ANY)],
        out_specs=pl.BlockSpec(memory_space=pltpu.VMEM),
        scratch_shapes=[
            pltpu.VMEM((snap, depth), bf16),
            pltpu.VMEM((16, depth), bf16),
            pltpu.VMEM((16, depth // PIECES), bf16),
            pltpu.VMEM((16, depth // PIECES), bf16),
            pltpu.VMEM((SLOT, depth), bf16),
            pltpu.VMEM((groups, CHIPS, 2, mine, TILE), f32),
            pltpu.VMEM((CHIPS, 2, mine, SLOT), f32),
            pltpu.VMEM((groups, CHIPS, mine, TILE), f32),
            pltpu.VMEM((CHIPS, mine, SLOT), f32),
            pltpu.VMEM((groups, CHIPS, mine, TILE), f32),
            pltpu.VMEM((CHIPS, mine, SLOT), f32),
            pltpu.VMEM((groups, CHIPS, mine, TILE), f32),
            pltpu.VMEM((CHIPS, mine, SLOT), f32),
            dma((groups,)),
            dma,
            dma((CHUNKS,)),
            dma((CHUNKS,)),
            dma((2,)),
            dma((groups + 1,)),
            dma((groups + 1,)),
            dma((groups + 1, CHIPS)),
            dma((groups + 1, CHIPS)),
        ],
        compiler_params=pltpu.CompilerParams(
            collective_id=0, has_side_effects=True, vmem_limit_bytes=56 * 2**20
        ),
        name="lagged_gram",
    )(snapshots)
    return summed[:, :columns] * (1.0 / total_rows)


def solution(mesh):
    return jax.shard_map(
        on_device,
        mesh=mesh,
        in_specs=(P("tm", "row"),),
        out_specs=P(("tm", "row"), None),
        check_vma=False,
    )
```

time: 257 us -> 85.8 us (0.33)
  the two profiles are of different devices: /device:TPU:1 before, /device:TPU:56 now
where the time goes in v1:
time: 85.8 us; the launch traced here: 85.7 us
  Pallas kernels  84 us (98%)
  other arithmetic  1.7 us (2%)
    pallas_call x1, Pallas kernels, on_device(): pl.pallas_call(kernel, out_shape=jax.ShapeDtypeStruct((mine, snap + SLOT)...  84 us

profile of v1, /device:TPU:56, one launch (start us, length us, event | category | flops | bytes accessed | tf_op | source)
XLA Modules:
  0.0 85.7 jit_solution(7030259681532252536)
XLA Ops:
  0.0 84.0 %lagged_gram.1 = f32[64,1152]{1,0:T(8,128)} custom-call(bf16[1024,10240]{1,0:T(8,128)(2,1)} %a_ref.1), custom_call_target="tpu_custom_call" | custom-call | tf_op jit(solution)/shard_map/lagged_gram/pallas_call | solution.py:265
  84.0 1.7 %slice_multiply_fusion = f32[64,1123]{1,0:T(8,128)} fusion(f32[64,1152]{1,0:T(8,128)} %lagged_gram.1), kind=kLoop, calls=%fused_computation | loop fusion | flops 71872 | bytes 574976 | tf_op jit(solution)/shard_map/mul | solution.py:299

commit v2 on v0

v2 whole, which is shorter than its diff:
```python
import jax
import jax.numpy as jnp
from jax import lax
from jax.experimental import pallas as pl
from jax.experimental.pallas import tpu as pltpu
from jax.sharding import PartitionSpec as P

MESH = pl.DeviceIdType.MESH
LAG = 100
CHIPS = 8
TM = 8
TILE = 256
GROUPS = 4
BULK = 96
REST = LAG - 1 - BULK
PIECES = 5
SLOT = 128
CHUNKS = 20
LONG = 5
HALF = CHUNKS // 2
NEAR = CHUNKS - LONG
NT = (((1,), (1,)), ((), ()))


def outer(left, right):
    return lax.dot_general(left, right, NT, preferred_element_type=jnp.float32)


def loop(start, stop, body):
    def step(i, carry):
        body(i)
        return carry

    lax.fori_loop(start, stop, step, 0)


def kernel(
    a_ref,
    out_ref,
    a_v,
    tail_v,
    packed_src,
    packed_dst,
    strip,
    first,
    second,
    via,
    acc,
    acc_s,
    pair,
    pair_s,
    part,
    part_s,
    got_x,
    mid,
    got_z,
    got_s,
    load_sem,
    tail_sem,
    strip_send,
    strip_recv,
    packed_sem,
    first_sem,
    second_sem,
    third_send,
    via_sem,
    away_send,
    pair_sem,
    x_sem,
    z_sem,
    s_sem,
):
    depth = a_v.shape[1]
    row, tm = lax.axis_index("row"), lax.axis_index("tm")
    chip, core = row // 2, row % 2
    zh, x = chip // 4, chip % 4
    zl, y = tm // 4, tm % 4
    partner = (chip * 2 + 1 - core, tm)
    before = (row, (tm + TM - 1) % TM)
    up = (row, zl * 4 + (y + 1) % 4)
    down = (row, zl * 4 + (y + 3) % 4)

    def peer(other):
        return (other * 2 + core, tm)

    def remote(src, dst, send, recv, device):
        return pltpu.make_async_remote_copy(
            src_ref=src,
            dst_ref=dst,
            send_sem=send,
            recv_sem=recv,
            device_id=device,
            device_id_type=MESH,
        )

    tail = pltpu.make_async_copy(a_ref.at[pl.ds(BULK, 16)], tail_v, tail_sem)
    tail.start()

    def load(block):
        rows = pl.ds(pl.multiple_of(block * TILE, TILE), TILE)
        return pltpu.make_async_copy(a_ref.at[rows], a_v.at[rows], load_sem.at[block])

    loop(0, GROUPS, lambda block: load(block).start())

    barrier = pltpu.get_barrier_semaphore()

    def greet(device):
        pl.semaphore_signal(barrier, inc=1, device_id=device, device_id_type=MESH)

    greet(up)
    greet(down)
    greet(partner)
    for d in range(1, CHIPS):
        greet(peer((chip + d) % CHIPS))

    @pl.when(tm == 0)
    def _():
        greet((row, 4))

    @pl.when(tm == 3)
    def _():
        greet((row, 4))

    @pl.when(tm == 4)
    def _():
        greet((row, 0))
        greet((row, 3))

    tail.wait()
    piece = depth // PIECES
    rows16 = lax.broadcasted_iota(jnp.int32, (16, piece), 0)
    packed = jnp.zeros((16, piece), jnp.float32)
    for p in range(PIECES):
        part_p = tail_v[:, p * piece : (p + 1) * piece].astype(jnp.float32)
        part_p = jnp.where(rows16 < REST, part_p, 0.0)
        packed += part_p if p == 0 else pltpu.roll(part_p, REST * p, 0)
    packed_src[...] = packed.astype(jnp.bfloat16)

    more = (tm == 0).astype(jnp.int32) + (tm == 3).astype(jnp.int32)
    more = more + 2 * (tm == 4).astype(jnp.int32)
    pl.semaphore_wait(barrier, CHIPS + 2 + more)

    width = depth // CHUNKS

    def cols(i):
        return pl.ds(pl.multiple_of(i * width, width), width)

    def source(i):
        return a_ref.at[pl.ds(0, BULK), cols(i)]

    def landing(i):
        return strip.at[pl.ds(0, BULK), cols(i)]

    def near(i):
        return remote(source(i), landing(i), strip_send.at[i], strip_recv.at[i], before)

    def hop1(k):
        dst = first.at[:, cols(k)]
        return remote(source(NEAR + k), dst, first_sem.at[0, k], first_sem.at[1, k], up)

    def hop2(k):
        src, dst = first.at[:, cols(k)], second.at[:, cols(k)]
        return remote(src, dst, second_sem.at[0, k], second_sem.at[1, k], up)

    def hop3(k):
        src, dst = second.at[:, cols(k)], landing(NEAR + k)
        return remote(src, dst, third_send.at[k], strip_recv.at[NEAR + k], up)

    def via1(k):
        dst = via.at[:, cols(k)]
        return remote(source(HALF + k), dst, via_sem.at[0, k], via_sem.at[1, k], (row, 0))

    def via2(k):
        src, dst = via.at[:, cols(k)], landing(HALF + k)
        return remote(src, dst, away_send.at[k], strip_recv.at[HALF + k], (row, 3))

    send_packed = remote(
        packed_src, packed_dst, packed_sem.at[0], packed_sem.at[1], before
    )
    sends1, sends2, sends3 = y != 0, y != 1, y != 2

    @pl.when(tm > 0)
    def _():
        send_packed.start()

    def begin(i):
        @pl.when(tm > 0)
        def _():
            near(i).start()

        @pl.when(sends1 & (i < LONG))
        def _():
            hop1(i).start()

        @pl.when(tm == 4)
        def _():
            via1(i).start()

    def begin_rest(i):
        @pl.when((tm > 0) & (tm != 4))
        def _():
            near(i).start()

    loop(0, HALF, begin)
    loop(HALF, NEAR, begin_rest)

    acc_s[...] = jnp.zeros_like(acc_s)
    strip[pl.ds(112, 16), :] = jnp.zeros((16, depth), jnp.bfloat16)

    def forward(p):
        @pl.when(sends2 & (p < LONG))
        def _():
            hop1(p).wait_recv()
            hop2(p).start()

        @pl.when(sends3 & (p >= LONG))
        def _():
            hop2(p - LONG).wait_recv()
            hop3(p - LONG).start()

        @pl.when(tm == 0)
        def _():
            via1(p).wait_recv()
            via2(p).start()

    def pair_of(g):
        src = acc.at[g, :, 1 - core]
        return remote(src, pair.at[g], pair_sem.at[0, g], pair_sem.at[1, g], partner)

    def x_of(g, d):
        other = (x + d) % 4
        src, dst = part.at[g, :, other], got_x.at[g, d]
        return remote(
            src, dst, x_sem.at[0, g, d], x_sem.at[1, g, d], peer(zh * 4 + other)
        )

    def z_of(g):
        src, dst = mid.at[g, 1 - zh], got_z.at[g]
        return remote(
            src, dst, z_sem.at[0, g], z_sem.at[1, g], peer((1 - zh) * 4 + x)
        )

    def exchange_x(g):
        pair_of(g).wait_recv()
        for q in range(CHIPS):
            part[g, q // 4, q % 4] = acc[g, q, core] + pair[g, q]
        for d in (2, 1, 3):
            x_of(g, d).start()

    def exchange_z(g):
        for d in (1, 3, 2):
            x_of(g, d).wait_recv()
        for half in range(2):
            total = part[g, half, x]
            for d in range(1, 4):
                total += got_x[g, d, half]
            mid[g, half] = total
        z_of(g).start()

    def finish(g):
        z_of(g).wait_recv()
        columns = pl.ds(pl.multiple_of(g * TILE, TILE), TILE)
        out_ref[:, columns] = mid[g, zh] + got_z[g]

    def one_tile(t):
        def past(bound):
            return (t >= bound).astype(jnp.int32)

        left = past(4) + past(7) + past(9)
        low = t - 4 * past(4) - 3 * past(7) - 2 * past(9) + left

        @pl.when(t < GROUPS)
        def _():
            load(t).wait()

        rows = pl.ds(pl.multiple_of(low * TILE, TILE), TILE)
        columns = pl.ds(pl.multiple_of(left * TILE, TILE), TILE)
        tile = outer(a_v[rows, :], a_v[columns, :])
        acc[left, pl.ds(low * 2, 2)] = tile.reshape(2, 2, 64, TILE)
        acc[low, pl.ds(left * 2, 2)] = tile.T.reshape(2, 2, 64, TILE)

        @pl.when(low == GROUPS - 1)
        def _():
            pair_of(left).start()

        @pl.when((t != 0) & (t != 3) & (t != 7))
        def _():
            forward(t - 1 - past(4) - past(8))

        @pl.when((t == 4) | (t == 7) | (t == 9))
        def _():
            exchange_x(past(5) + past(8))

    loop(0, 10, one_tile)

    def strip_chunk(i):
        near(i).wait_recv()
        tile = outer(a_v[:, cols(i)], strip[:, cols(i)])
        acc_s[...] += tile.reshape(CHIPS, 2, 64, SLOT)

    @pl.when(tm < TM - 1)
    def _():
        send_packed.wait_recv()
        packed = packed_dst[...].astype(jnp.float32)
        for p in range(PIECES):
            part_p = packed if p == 0 else pltpu.roll(packed, 16 - REST * p, 0)
            part_p = jnp.where(rows16 < REST, part_p, 0.0)
            strip[pl.ds(BULK, 16), pl.ds(p * piece, piece)] = part_p.astype(
                jnp.bfloat16
            )

    def one_chunk(pos):
        @pl.when(tm < TM - 1)
        def _():
            late = pos - HALF
            chunk = jnp.where(late < 0, pos, HALF + late // 2 + LONG * (late % 2))
            strip_chunk(chunk)

        @pl.when((pos == 0) | (pos == 2) | (pos == 6))
        def _():
            forward(7 + (pos > 1).astype(jnp.int32) + (pos > 5).astype(jnp.int32))

        @pl.when(pos == 1)
        def _():
            exchange_x(GROUPS - 1)

        @pl.when((pos == 3) | (pos == 8) | (pos == 14))
        def _():
            exchange_z((pos > 4).astype(jnp.int32) + (pos > 10).astype(jnp.int32))

    loop(0, CHUNKS, one_chunk)

    def s_pair():
        src = acc_s.at[:, 1 - core]
        return remote(src, pair_s, s_sem.at[0, 0], s_sem.at[1, 0], partner)

    def s_of(d):
        other = (chip + d) % CHIPS
        src, dst = part_s.at[other], got_s.at[d]
        return remote(src, dst, s_sem.at[0, d], s_sem.at[1, d], peer(other))

    s_pair().start()
    exchange_z(GROUPS - 1)
    s_pair().wait_recv()
    for q in range(CHIPS):
        part_s[q] = acc_s[q, core] + pair_s[q]
    for d in range(1, CHIPS):
        s_of(d).start()
    loop(0, GROUPS, finish)
    total = part_s[chip]
    for d in range(1, CHIPS):
        s_of(d).wait_recv()
        total += got_s[d]
    out_ref[:, pl.ds(GROUPS * TILE, SLOT)] = total

    @pl.when(tm > 0)
    def _():
        send_packed.wait_send()

    def ended(i):
        @pl.when((tm > 0) & ((tm != 4) | (i < HALF)))
        def _():
            near(i).wait_send()

    loop(0, NEAR, ended)

    def ended_long(k):
        @pl.when(sends1)
        def _():
            hop1(k).wait_send()

        @pl.when(sends2)
        def _():
            hop2(k).wait_send()

        @pl.when(sends3)
        def _():
            hop3(k).wait_send()

    loop(0, LONG, ended_long)

    def ended_via(k):
        @pl.when(tm == 4)
        def _():
            via1(k).wait_send()

        @pl.when(tm == 0)
        def _():
            via2(k).wait_send()

    loop(0, HALF, ended_via)

    def ended_group(g):
        pair_of(g).wait_send()
        z_of(g).wait_send()
        for d in range(1, 4):
            x_of(g, d).wait_send()

    loop(0, GROUPS, ended_group)
    s_pair().wait_send()
    for d in range(1, CHIPS):
        s_of(d).wait_send()


def on_device(snapshots):
    snap, depth = snapshots.shape
    mine = snap // lax.axis_size("row")
    total_rows = depth * lax.axis_size("row")
    columns = snap + LAG - 1
    width = depth // CHUNKS
    f32, bf16 = jnp.float32, jnp.bfloat16
    dma = pltpu.SemaphoreType.DMA
    summed = pl.pallas_call(
        kernel,
        out_shape=jax.ShapeDtypeStruct((mine, snap + SLOT), f32),
        in_specs=[pl.BlockSpec(memory_space=pl.ANY)],
        out_specs=pl.BlockSpec(memory_space=pltpu.VMEM),
        scratch_shapes=[
            pltpu.VMEM((snap, depth), bf16),
            pltpu.VMEM((16, depth), bf16),
            pltpu.VMEM((16, depth // PIECES), bf16),
            pltpu.VMEM((16, depth // PIECES), bf16),
            pltpu.VMEM((SLOT, depth), bf16),
            pltpu.VMEM((BULK, LONG * width), bf16),
            pltpu.VMEM((BULK, LONG * width), bf16),
            pltpu.VMEM((BULK, HALF * width), bf16),
            pltpu.VMEM((GROUPS, CHIPS, 2, mine, TILE), f32),
            pltpu.VMEM((CHIPS, 2, mine, SLOT), f32),
            pltpu.VMEM((GROUPS, CHIPS, mine, TILE), f32),
            pltpu.VMEM((CHIPS, mine, SLOT), f32),
            pltpu.VMEM((GROUPS, 2, 4, mine, TILE), f32),
            pltpu.VMEM((CHIPS, mine, SLOT), f32),
            pltpu.VMEM((GROUPS, 4, 2, mine, TILE), f32),
            pltpu.VMEM((GROUPS, 2, mine, TILE), f32),
            pltpu.VMEM((GROUPS, mine, TILE), f32),
            pltpu.VMEM((CHIPS, mine, SLOT), f32),
            dma((GROUPS,)),
            dma,
            dma((CHUNKS,)),
            dma((CHUNKS,)),
            dma((2,)),
            dma((2, LONG)),
            dma((2, LONG)),
            dma((LONG,)),
            dma((2, HALF)),
            dma((HALF,)),
            dma((2, GROUPS)),
            dma((2, GROUPS, 4)),
            dma((2, GROUPS)),
            dma((2, CHIPS)),
        ],
        compiler_params=pltpu.CompilerParams(
            collective_id=0, has_side_effects=True, vmem_limit_bytes=56 * 2**20
        ),
        name="lagged_gram",
    )(snapshots)
    return summed[:, :columns] * (1.0 / total_rows)


def solution(mesh):
    return jax.shard_map(
        on_device,
        mesh=mesh,
        in_specs=(P("tm", "row"),),
        out_specs=P(("tm", "row"), None),
        check_vma=False,
    )
```

time: 257 us -> 53.6 us (0.21)
  waiting for transfers between devices: 205 us -> 0 us
  Pallas kernels: 0 us -> 51.8 us
  matrix products: 33.6 us -> 0 us
  between operations: 13.4 us -> 0.01 us
    psum x1 -> x0, waiting for transfers between devices: 157 us -> none  [on_device(): summed = lax.psum(lagged(snapshots, extended), 'row')]
    pallas_call x0 -> x1, Pallas kernels: none -> 51.8 us  [on_device(): pl.pallas_call(kernel, out_shape=jax.ShapeDtypeStruct((mine, snap + SLOT)...]
    ppermute x1 -> x0, waiting for transfers between devices: 48.4 us -> none  [from_behind(): return lax.ppermute(block, axis, route)]
    dot_general x1 -> x0, matrix products: 33.6 us -> none  [lagged(): return jnp.dot(left, right.T, preferred_element_type=jnp.float32)]
  transfers between devices with their start and end apart: 2 -> 0, of which waited for: 2 -> 0; matrix products, arithmetic and copies ran while one was open for 0% -> 0% of each run, Pallas kernels for 0% -> 0%
where the time goes in v2:
time: 53.6 us; the launch traced here: 53.5 us
  Pallas kernels  51.8 us (97%)
  other arithmetic  1.7 us (3%)
    pallas_call x1, Pallas kernels, on_device(): pl.pallas_call(kernel, out_shape=jax.ShapeDtypeStruct((mine, snap + SLOT)...  51.8 us
    mul x1, other arithmetic, on_device(): return summed[:, :columns] * (1.0 / total_rows)  1.7 us

profile of v2, /device:TPU:1, one launch (start us, length us, event | category | flops | bytes accessed | tf_op | source)
XLA Modules:
  0.0 53.5 jit_solution(17027703379663839609)
XLA Ops:
  0.0 51.8 %lagged_gram.1 = f32[64,1152]{1,0:T(8,128)} custom-call(bf16[1024,10240]{1,0:T(8,128)(2,1)} %a_ref.1), custom_call_target="tpu_custom_call" | custom-call | tf_op jit(solution)/shard_map/lagged_gram/pallas_call | solution.py:413
  51.8 1.7 %slice_multiply_fusion = f32[64,1123]{1,0:T(8,128)} fusion(f32[64,1152]{1,0:T(8,128)} %lagged_gram.1), kind=kLoop, calls=%fused_computation | loop fusion | flops 71872 | bytes 574976 | tf_op jit(solution)/shard_map/mul | solution.py:457

commit v3 on v2

--- a/solution.py
+++ b/solution.py
@@ -38,7 +38,6 @@
     a_ref,
     out_ref,
     a_v,
-    tail_v,
     packed_src,
     packed_dst,
     strip,
@@ -54,6 +53,8 @@
     got_x,
     mid,
     got_z,
+    mid4,
+    got_z4,
     got_s,
     load_sem,
     tail_sem,
@@ -93,14 +94,17 @@
             device_id_type=MESH,
         )
 
-    tail = pltpu.make_async_copy(a_ref.at[pl.ds(BULK, 16)], tail_v, tail_sem)
-    tail.start()
+    def load_rows(start, size, sem):
+        rows = pl.ds(start, size)
+        return pltpu.make_async_copy(a_ref.at[rows], a_v.at[rows], sem)
+
+    head = load_rows(0, SLOT, tail_sem.at[0])
+    rest = load_rows(SLOT, TILE - SLOT, tail_sem.at[1])
+    head.start()
 
     def load(block):
         rows = pl.ds(pl.multiple_of(block * TILE, TILE), TILE)
         return pltpu.make_async_copy(a_ref.at[rows], a_v.at[rows], load_sem.at[block])
-
-    loop(0, GROUPS, lambda block: load(block).start())
 
     barrier = pltpu.get_barrier_semaphore()
 
@@ -126,86 +130,92 @@
         greet((row, 0))
         greet((row, 3))
 
-    tail.wait()
+    head.wait()
+    rest.start()
+    loop(1, GROUPS, lambda block: load(block).start())
+    more = (tm == 0).astype(jnp.int32) + (tm == 3).astype(jnp.int32)
+    more = more + 2 * (tm == 4).astype(jnp.int32)
+    pl.semaphore_wait(barrier, CHIPS + 2 + more)
+
+    width = depth // CHUNKS
+
+    def cols(i):
+        return pl.ds(pl.multiple_of(i * width, width), width)
+
+    def source(i):
+        return a_v.at[pl.ds(0, BULK), cols(i)]
+
+    def landing(i):
+        return strip.at[i, pl.ds(0, BULK)]
+
+    def near(i):
+        return remote(source(i), landing(i), strip_send.at[i], strip_recv.at[i], before)
+
+    def hop1(k):
+        dst = first.at[k]
+        return remote(source(NEAR + k), dst, first_sem.at[0, k], first_sem.at[1, k], up)
+
+    def hop2(k):
+        src, dst = first.at[k], second.at[k]
+        return remote(src, dst, second_sem.at[0, k], second_sem.at[1, k], up)
+
+    def hop3(k):
+        src, dst = second.at[k], landing(NEAR + k)
+        return remote(src, dst, third_send.at[k], strip_recv.at[NEAR + k], up)
+
+    def via1(k):
+        dst = via.at[k]
+        return remote(source(HALF + k), dst, via_sem.at[0, k], via_sem.at[1, k], (row, 0))
+
+    def via2(k):
+        src, dst = via.at[k], landing(HALF + k)
+        return remote(src, dst, away_send.at[k], strip_recv.at[HALF + k], (row, 3))
+
+    send_packed = remote(
+        packed_src, packed_dst, packed_sem.at[0], packed_sem.at[1], before
+    )
+    sends1, sends2, sends3 = y != 0, y != 1, y != 2
+
+    def begin(i):
+        @pl.when(tm > 0)
+        def _():
+            near(i).start()
+
+        @pl.when(sends1 & (i < LONG))
+        def _():
+            hop1(i).start()
+
+        @pl.when(tm == 4)
+        def _():
+            via1(i).start()
+
+    def begin_rest(i):
+        @pl.when((tm > 0) & (tm != 4))
+        def _():
+            near(i).start()
+
+    loop(0, 2, begin)
+
     piece = depth // PIECES
     rows16 = lax.broadcasted_iota(jnp.int32, (16, piece), 0)
     packed = jnp.zeros((16, piece), jnp.float32)
     for p in range(PIECES):
-        part_p = tail_v[:, p * piece : (p + 1) * piece].astype(jnp.float32)
+        part_p = a_v[BULK : BULK + 16, p * piece : (p + 1) * piece].astype(jnp.float32)
         part_p = jnp.where(rows16 < REST, part_p, 0.0)
         packed += part_p if p == 0 else pltpu.roll(part_p, REST * p, 0)
     packed_src[...] = packed.astype(jnp.bfloat16)
 
-    more = (tm == 0).astype(jnp.int32) + (tm == 3).astype(jnp.int32)
-    more = more + 2 * (tm == 4).astype(jnp.int32)
-    pl.semaphore_wait(barrier, CHIPS + 2 + more)
-
-    width = depth // CHUNKS
-
-    def cols(i):
-        return pl.ds(pl.multiple_of(i * width, width), width)
-
-    def source(i):
-        return a_ref.at[pl.ds(0, BULK), cols(i)]
-
-    def landing(i):
-        return strip.at[pl.ds(0, BULK), cols(i)]
-
-    def near(i):
-        return remote(source(i), landing(i), strip_send.at[i], strip_recv.at[i], before)
-
-    def hop1(k):
-        dst = first.at[:, cols(k)]
-        return remote(source(NEAR + k), dst, first_sem.at[0, k], first_sem.at[1, k], up)
-
-    def hop2(k):
-        src, dst = first.at[:, cols(k)], second.at[:, cols(k)]
-        return remote(src, dst, second_sem.at[0, k], second_sem.at[1, k], up)
-
-    def hop3(k):
-        src, dst = second.at[:, cols(k)], landing(NEAR + k)
-        return remote(src, dst, third_send.at[k], strip_recv.at[NEAR + k], up)
-
-    def via1(k):
-        dst = via.at[:, cols(k)]
-        return remote(source(HALF + k), dst, via_sem.at[0, k], via_sem.at[1, k], (row, 0))
-
-    def via2(k):
-        src, dst = via.at[:, cols(k)], landing(HALF + k)
-        return remote(src, dst, away_send.at[k], strip_recv.at[HALF + k], (row, 3))
-
-    send_packed = remote(
-        packed_src, packed_dst, packed_sem.at[0], packed_sem.at[1], before
-    )
-    sends1, sends2, sends3 = y != 0, y != 1, y != 2
-
     @pl.when(tm > 0)
     def _():
         send_packed.start()
 
-    def begin(i):
-        @pl.when(tm > 0)
-        def _():
-            near(i).start()
-
-        @pl.when(sends1 & (i < LONG))
-        def _():
-            hop1(i).start()
-
-        @pl.when(tm == 4)
-        def _():
-            via1(i).start()
-
-    def begin_rest(i):
-        @pl.when((tm > 0) & (tm != 4))
-        def _():
-            near(i).start()
-
-    loop(0, HALF, begin)
+    loop(2, HALF, begin)
     loop(HALF, NEAR, begin_rest)
 
     acc_s[...] = jnp.zeros_like(acc_s)
-    strip[pl.ds(112, 16), :] = jnp.zeros((16, depth), jnp.bfloat16)
+    strip[:, BULK + 16 :, :] = jnp.zeros(
+        (CHUNKS, SLOT - BULK - 16, width), jnp.bfloat16
+    )
 
     def forward(p):
         @pl.when(sends2 & (p < LONG))
@@ -240,10 +250,15 @@
             src, dst, z_sem.at[0, g], z_sem.at[1, g], peer((1 - zh) * 4 + x)
         )
 
-    def exchange_x(g):
+    last = GROUPS - 1
+
+    def sum_pair(g):
         pair_of(g).wait_recv()
         for q in range(CHIPS):
             part[g, q // 4, q % 4] = acc[g, q, core] + pair[g, q]
+
+    def exchange_x(g):
+        sum_pair(g)
         for d in (2, 1, 3):
             x_of(g, d).start()
 
@@ -262,6 +277,40 @@
         columns = pl.ds(pl.multiple_of(g * TILE, TILE), TILE)
         out_ref[:, columns] = mid[g, zh] + got_z[g]
 
+    def z_first():
+        src = part.at[last, 1 - zh]
+        return remote(
+            src, got_z4, z_sem.at[0, last], z_sem.at[1, last], peer((1 - zh) * 4 + x)
+        )
+
+    def x_last(d):
+        other = (x + d) % 4
+        return remote(
+            mid4.at[other],
+            got_x.at[last, d, 0],
+            x_sem.at[0, last, d],
+            x_sem.at[1, last, d],
+            peer(zh * 4 + other),
+        )
+
+    def last_z():
+        sum_pair(last)
+        z_first().start()
+
+    def last_x():
+        z_first().wait_recv()
+        for q in range(4):
+            mid4[q] = part[last, zh, q] + got_z4[q]
+        for d in (2, 1, 3):
+            x_last(d).start()
+
+    def last_finish():
+        total = mid4[x]
+        for d in (1, 3, 2):
+            x_last(d).wait_recv()
+            total += got_x[last, d, 0]
+        out_ref[:, pl.ds(last * TILE, TILE)] = total
+
     def one_tile(t):
         def past(bound):
             return (t >= bound).astype(jnp.int32)
@@ -269,7 +318,11 @@
         left = past(4) + past(7) + past(9)
         low = t - 4 * past(4) - 3 * past(7) - 2 * past(9) + left
 
-        @pl.when(t < GROUPS)
+        @pl.when(t == 0)
+        def _():
+            rest.wait()
+
+        @pl.when((t > 0) & (t < GROUPS))
         def _():
             load(t).wait()
 
@@ -295,7 +348,7 @@
 
     def strip_chunk(i):
         near(i).wait_recv()
-        tile = outer(a_v[:, cols(i)], strip[:, cols(i)])
+        tile = outer(a_v[:, cols(i)], strip[i])
         acc_s[...] += tile.reshape(CHIPS, 2, 64, SLOT)
 
     @pl.when(tm < TM - 1)
@@ -305,9 +358,11 @@
         for p in range(PIECES):
             part_p = packed if p == 0 else pltpu.roll(packed, 16 - REST * p, 0)
             part_p = jnp.where(rows16 < REST, part_p, 0.0)
-            strip[pl.ds(BULK, 16), pl.ds(p * piece, piece)] = part_p.astype(
-                jnp.bfloat16
-            )
+            part_p = part_p.astype(jnp.bfloat16)
+            for k in range(piece // width):
+                strip[p * (piece // width) + k, BULK : BULK + 16] = part_p[
+                    :, k * width : (k + 1) * width
+                ]
 
     def one_chunk(pos):
         @pl.when(tm < TM - 1)
@@ -322,7 +377,11 @@
 
         @pl.when(pos == 1)
         def _():
-            exchange_x(GROUPS - 1)
+            last_z()
+
+        @pl.when(pos == 12)
+        def _():
+            last_x()
 
         @pl.when((pos == 3) | (pos == 8) | (pos == 14))
         def _():
@@ -335,20 +394,20 @@
         return remote(src, pair_s, s_sem.at[0, 0], s_sem.at[1, 0], partner)
 
     def s_of(d):
-        other = (chip + d) % CHIPS
+        other = (zh + d // 4) % 2 * 4 + (x + d) % 4
         src, dst = part_s.at[other], got_s.at[d]
         return remote(src, dst, s_sem.at[0, d], s_sem.at[1, d], peer(other))
 
     s_pair().start()
-    exchange_z(GROUPS - 1)
     s_pair().wait_recv()
     for q in range(CHIPS):
         part_s[q] = acc_s[q, core] + pair_s[q]
-    for d in range(1, CHIPS):
+    for d in (6, 5, 7, 2, 4, 1, 3):
         s_of(d).start()
-    loop(0, GROUPS, finish)
+    loop(0, last, finish)
+    last_finish()
     total = part_s[chip]
-    for d in range(1, CHIPS):
+    for d in (1, 3, 4, 2, 5, 7, 6):
         s_of(d).wait_recv()
         total += got_s[d]
     out_ref[:, pl.ds(GROUPS * TILE, SLOT)] = total
@@ -391,12 +450,15 @@
     loop(0, HALF, ended_via)
 
     def ended_group(g):
-        pair_of(g).wait_send()
         z_of(g).wait_send()
         for d in range(1, 4):
             x_of(g, d).wait_send()
 
-    loop(0, GROUPS, ended_group)
+    loop(0, last, ended_group)
+    z_first().wait_send()
+    for d in range(1, 4):
+        x_last(d).wait_send()
+    loop(0, GROUPS, lambda g: pair_of(g).wait_send())
     s_pair().wait_send()
     for d in range(1, CHIPS):
         s_of(d).wait_send()
@@ -417,13 +479,12 @@
         out_specs=pl.BlockSpec(memory_space=pltpu.VMEM),
         scratch_shapes=[
             pltpu.VMEM((snap, depth), bf16),
-            pltpu.VMEM((16, depth), bf16),
             pltpu.VMEM((16, depth // PIECES), bf16),
             pltpu.VMEM((16, depth // PIECES), bf16),
-            pltpu.VMEM((SLOT, depth), bf16),
-            pltpu.VMEM((BULK, LONG * width), bf16),
-            pltpu.VMEM((BULK, LONG * width), bf16),
-            pltpu.VMEM((BULK, HALF * width), bf16),
+            pltpu.VMEM((CHUNKS, SLOT, width), bf16),
+            pltpu.VMEM((LONG, BULK, width), bf16),
+            pltpu.VMEM((LONG, BULK, width), bf16),
+            pltpu.VMEM((HALF, BULK, width), bf16),
             pltpu.VMEM((GROUPS, CHIPS, 2, mine, TILE), f32),
             pltpu.VMEM((CHIPS, 2, mine, SLOT), f32),
             pltpu.VMEM((GROUPS, CHIPS, mine, TILE), f32),
@@ -433,9 +494,11 @@
             pltpu.VMEM((GROUPS, 4, 2, mine, TILE), f32),
             pltpu.VMEM((GROUPS, 2, mine, TILE), f32),
             pltpu.VMEM((GROUPS, mine, TILE), f32),
+            pltpu.VMEM((4, mine, TILE), f32),
+            pltpu.VMEM((4, mine, TILE), f32),
             pltpu.VMEM((CHIPS, mine, SLOT), f32),
             dma((GROUPS,)),
-            dma,
+            dma((2,)),
             dma((CHUNKS,)),
             dma((CHUNKS,)),
             dma((2,)),

time: 53.6 us -> 53.1 us (level)
  Pallas kernels: 51.8 us -> 51.2 us
where the time goes in v3:
time: 53.1 us; the launch traced here: 52.9 us
  Pallas kernels  51.2 us (96%)
  other arithmetic  1.7 us (3%)
    pallas_call x1, Pallas kernels, on_device(): pl.pallas_call(kernel, out_shape=jax.ShapeDtypeStruct((mine, snap + SLOT)...  51.2 us
    mul x1, other arithmetic, on_device(): return summed[:, :columns] * (1.0 / total_rows)  1.7 us

profile of v3, /device:TPU:1, one launch (start us, length us, event | category | flops | bytes accessed | tf_op | source)
XLA Modules:
  0.0 52.9 jit_solution(14966451748068312)
XLA Ops:
  0.0 51.2 %lagged_gram.1 = f32[64,1152]{1,0:T(8,128)} custom-call(bf16[1024,10240]{1,0:T(8,128)(2,1)} %a_ref.1), custom_call_target="tpu_custom_call" | custom-call | tf_op jit(solution)/shard_map/lagged_gram/pallas_call | solution.py:475
  51.2 1.7 %slice_multiply_fusion = f32[64,1123]{1,0:T(8,128)} fusion(f32[64,1152]{1,0:T(8,128)} %lagged_gram.1), kind=kLoop, calls=%fused_computation | loop fusion | flops 71872 | bytes 574976 | tf_op jit(solution)/shard_map/mul | solution.py:520

commit v4 on v3

--- a/solution.py
+++ b/solution.py
@@ -146,7 +146,8 @@
         return a_v.at[pl.ds(0, BULK), cols(i)]
 
     def landing(i):
-        return strip.at[i, pl.ds(0, BULK)]
+        half = pl.ds(pl.multiple_of(i % 2 * width, width), width)
+        return strip.at[i // 2, pl.ds(0, BULK), half]
 
     def near(i):
         return remote(source(i), landing(i), strip_send.at[i], strip_recv.at[i], before)
@@ -214,7 +215,7 @@
 
     acc_s[...] = jnp.zeros_like(acc_s)
     strip[:, BULK + 16 :, :] = jnp.zeros(
-        (CHUNKS, SLOT - BULK - 16, width), jnp.bfloat16
+        (CHUNKS // 2, SLOT - BULK - 16, 2 * width), jnp.bfloat16
     )
 
     def forward(p):
@@ -348,7 +349,17 @@
 
     def strip_chunk(i):
         near(i).wait_recv()
-        tile = outer(a_v[:, cols(i)], strip[i])
+        tile = outer(
+            a_v[:, cols(i)],
+            strip[i // 2, :, pl.ds(pl.multiple_of(i % 2 * width, width), width)],
+        )
+        acc_s[...] += tile.reshape(CHIPS, 2, 64, SLOT)
+
+    def strip_double(i):
+        near(2 * i).wait_recv()
+        near(2 * i + 1).wait_recv()
+        wide = pl.ds(pl.multiple_of(i * 2 * width, 2 * width), 2 * width)
+        tile = outer(a_v[:, wide], strip[i])
         acc_s[...] += tile.reshape(CHIPS, 2, 64, SLOT)
 
     @pl.when(tm < TM - 1)
@@ -359,17 +370,20 @@
             part_p = packed if p == 0 else pltpu.roll(packed, 16 - REST * p, 0)
             part_p = jnp.where(rows16 < REST, part_p, 0.0)
             part_p = part_p.astype(jnp.bfloat16)
-            for k in range(piece // width):
-                strip[p * (piece // width) + k, BULK : BULK + 16] = part_p[
-                    :, k * width : (k + 1) * width
+            for k in range(2):
+                strip[2 * p + k, BULK : BULK + 16] = part_p[
+                    :, k * 2 * width : (k + 1) * 2 * width
                 ]
 
     def one_chunk(pos):
-        @pl.when(tm < TM - 1)
+        @pl.when((tm < TM - 1) & (pos < HALF) & (pos % 2 == 1))
+        def _():
+            strip_double(pos // 2)
+
+        @pl.when((tm < TM - 1) & (pos >= HALF))
         def _():
             late = pos - HALF
-            chunk = jnp.where(late < 0, pos, HALF + late // 2 + LONG * (late % 2))
-            strip_chunk(chunk)
+            strip_chunk(HALF + late // 2 + LONG * (1 - late % 2))
 
         @pl.when((pos == 0) | (pos == 2) | (pos == 6))
         def _():
@@ -481,7 +495,7 @@
             pltpu.VMEM((snap, depth), bf16),
             pltpu.VMEM((16, depth // PIECES), bf16),
             pltpu.VMEM((16, depth // PIECES), bf16),
-            pltpu.VMEM((CHUNKS, SLOT, width), bf16),
+            pltpu.VMEM((CHUNKS // 2, SLOT, 2 * width), bf16),
             pltpu.VMEM((LONG, BULK, width), bf16),
             pltpu.VMEM((LONG, BULK, width), bf16),
             pltpu.VMEM((HALF, BULK, width), bf16),

time: 53.1 us -> 53.1 us (level)
  no operation moved by 1% of the time
where the time goes in v4:
time: 53.1 us; the launch traced here: 53 us
  Pallas kernels  51.3 us (97%)
  other arithmetic  1.7 us (3%)
    pallas_call x1, Pallas kernels, on_device(): pl.pallas_call(kernel, out_shape=jax.ShapeDtypeStruct((mine, snap + SLOT)...  51.3 us
    mul x1, other arithmetic, on_device(): return summed[:, :columns] * (1.0 / total_rows)  1.7 us

profile of v4, /device:TPU:1, one launch (start us, length us, event | category | flops | bytes accessed | tf_op | source)
XLA Modules:
  0.0 53.0 jit_solution(9450130736446697469)
XLA Ops:
  0.0 51.3 %lagged_gram.1 = f32[64,1152]{1,0:T(8,128)} custom-call(bf16[1024,10240]{1,0:T(8,128)(2,1)} %a_ref.1), custom_call_target="tpu_custom_call" | custom-call | tf_op jit(solution)/shard_map/lagged_gram/pallas_call | solution.py:489
  51.3 1.7 %slice_multiply_fusion = f32[64,1123]{1,0:T(8,128)} fusion(f32[64,1152]{1,0:T(8,128)} %lagged_gram.1), kind=kLoop, calls=%fused_computation | loop fusion | flops 71872 | bytes 574976 | tf_op jit(solution)/shard_map/mul | solution.py:534

commit v5 on v4

--- a/solution.py
+++ b/solution.py
@@ -178,13 +178,13 @@
     sends1, sends2, sends3 = y != 0, y != 1, y != 2
 
     def begin(i):
+        @pl.when(sends1 & (i < LONG))
+        def _():
+            hop1(i).start()
+
         @pl.when(tm > 0)
         def _():
             near(i).start()
-
-        @pl.when(sends1 & (i < LONG))
-        def _():
-            hop1(i).start()
 
         @pl.when(tm == 4)
         def _():

time: 53.1 us -> 53.1 us (level)
  no operation moved by 1% of the time
where the time goes in v5:
time: 53.1 us; the launch traced here: 53 us
  Pallas kernels  51.3 us (97%)
  other arithmetic  1.7 us (3%)
    pallas_call x1, Pallas kernels, on_device(): pl.pallas_call(kernel, out_shape=jax.ShapeDtypeStruct((mine, snap + SLOT)...  51.3 us
    mul x1, other arithmetic, on_device(): return summed[:, :columns] * (1.0 / total_rows)  1.7 us

profile of v5, /device:TPU:1, one launch (start us, length us, event | category | flops | bytes accessed | tf_op | source)
XLA Modules:
  0.0 53.0 jit_solution(1272577998962078868)
XLA Ops:
  0.0 51.3 %lagged_gram.1 = f32[64,1152]{1,0:T(8,128)} custom-call(bf16[1024,10240]{1,0:T(8,128)(2,1)} %a_ref.1), custom_call_target="tpu_custom_call" | custom-call | tf_op jit(solution)/shard_map/lagged_gram/pallas_call | solution.py:489
  51.3 1.7 %slice_multiply_fusion = f32[64,1123]{1,0:T(8,128)} fusion(f32[64,1152]{1,0:T(8,128)} %lagged_gram.1), kind=kLoop, calls=%fused_computation | loop fusion | flops 71872 | bytes 574976 | tf_op jit(solution)/shard_map/mul | solution.py:534
